TPU v7x, 256 devices: a whole 4x4x8 slice. The times are simulated.
256 devices in a mesh: side: 2 (over x_lo), grp: 8 (over y, x_hi), shard: 16 (over z, core).
Axes of the slice: x: 4 (x_hi: 2, x_lo: 2; x = x_hi * 2 + x_lo), y: 4, z: 8, core: 2. Of those that a mesh axis runs over, the one named last changes fastest.
Arguments:
- queries: bfloat16 [512, 8192], P(('side', 'grp', 'shard')), may hold values from -80 to 80
- key_cache: bfloat16 [512, 192, 1024], P(('side', 'grp', 'shard')), may hold values from -4 to 4
- value_cache: bfloat16 [512, 192, 1024], P(('side', 'grp', 'shard')), may hold values from -8 to 8
- new_keys: bfloat16 [512, 1024], P(('side', 'grp', 'shard')), may hold values from -4 to 4
- new_values: bfloat16 [512, 1024], P(('side', 'grp', 'shard')), may hold values from -8 to 8
- lengths: int32 [512], P(('side', 'grp', 'shard')), may hold values from 1 to 192, as said below
- resid_in: bfloat16 [512, 8192], P(('side', 'grp', 'shard')), may hold values from -34 to 34
- norm_gain: bfloat16 [8192], replicated, may hold values from 0.099609375 to 1.8984375
- gate_weight: bfloat16 [53248, 8192], P(('side', 'grp', 'shard')), may hold values from -0.0625 to 0.0625
- up_weight: bfloat16 [53248, 8192], P(('side', 'grp', 'shard')), may hold values from -0.0625 to 0.0625
- down_weight: bfloat16 [53248, 8192], P(('side', 'grp', 'shard')), may hold values from -0.02734375 to 0.02734375
Outputs:
- attended: bfloat16 [512, 8192], P(('side', 'grp', 'shard'))
- ffn_out: bfloat16 [512, 8192], P(('side', 'grp', 'shard'))
Inputs may be any that keep to these rules, and one draw needn't show every extreme that they name: Request r's cache holds data in its first lengths[r] slots; some request has exactly 192.
All inputs are finite; a program needn't handle non-finite values.
Results may differ from a plain program's by a relative error of at most 0.013.
Values may be sent and summed in bfloat16 or wider, within the bound.
A program may use at most 128 MiB of HBM per device.

v0:
```python
import jax
import jax.numpy as jnp
from jax import lax
from jax.sharding import PartitionSpec as P

HD = 128
HEADS = 64
KVH = 8
CACHE = 192
BLOCK = 64


NEG_FILL = -1e30
EPSILON = 1e-05


def attend_requests(query, key_cache, value_cache, new_keys, new_values, lengths):
    req_count = query.shape[0]
    group_size = HEADS // KVH
    score_scale = HD ** (-0.5)
    query_heads = query.reshape(req_count, KVH, group_size, HD)
    cache_keys = key_cache.reshape(req_count, CACHE, KVH, HD)
    cache_values = value_cache.reshape(req_count, CACHE, KVH, HD)
    own_keys = new_keys.reshape(req_count, KVH, HD)
    own_values = new_values.reshape(req_count, KVH, 1, HD)
    own_score = (
        jnp.einsum("rkgh,rkh->rkg", query_heads, own_keys, preferred_element_type=jnp.float32)
        * score_scale
    )
    block_count = (jnp.max(lengths) + BLOCK - 1) // BLOCK

    def block_scores(block_index):
        keys_block = lax.dynamic_slice_in_dim(cache_keys, block_index * BLOCK, BLOCK, 1)
        scores = (
            jnp.einsum(
                "rkgh,rtkh->rkgt", query_heads, keys_block, preferred_element_type=jnp.float32
            )
            * score_scale
        )
        slots = block_index * BLOCK + jnp.arange(BLOCK, dtype=jnp.int32)
        is_valid = (slots[None, :] < lengths[:, None])[:, None, None, :]
        return (jnp.where(is_valid, scores, NEG_FILL), is_valid)

    def measure(block_index, carry):
        top_score, total_sum = carry
        scores, is_valid = block_scores(block_index)
        new_top = jnp.maximum(top_score, jnp.max(scores, axis=-1))
        weights = jnp.where(is_valid, jnp.exp(scores - new_top[..., None]), 0.0)
        return (new_top, total_sum * jnp.exp(top_score - new_top) + jnp.sum(weights, axis=-1))

    top_score, total_sum = lax.fori_loop(
        0, block_count, measure, (own_score, jnp.ones_like(own_score))
    )
    own_prob = (jnp.exp(own_score - top_score) / total_sum).astype(jnp.bfloat16)
    start_accum = own_prob.astype(jnp.float32)[..., None] * own_values.astype(jnp.float32)

    def accumulate(block_index, accum):
        scores, is_valid = block_scores(block_index)
        block_probs = (
            jnp.where(is_valid, jnp.exp(scores - top_score[..., None]), 0.0) / total_sum[..., None]
        ).astype(jnp.bfloat16)
        values_block = lax.dynamic_slice_in_dim(cache_values, block_index * BLOCK, BLOCK, 1)
        return accum + jnp.einsum(
            "rkgt,rtkh->rkgh", block_probs, values_block, preferred_element_type=jnp.float32
        )

    accum = lax.fori_loop(0, block_count, accumulate, start_accum)
    return accum.reshape(req_count, KVH * group_size * HD)


def local(
    queries,
    key_cache,
    value_cache,
    new_keys,
    new_values,
    lengths,
    resid_in,
    norm_gain,
    gate_weight,
    up_weight,
    down_weight,
):
    gain_f = norm_gain.astype(jnp.float32)
    mixed_heads = attend_requests(queries, key_cache, value_cache, new_keys, new_values, lengths)
    attended = (resid_in.astype(jnp.float32) + mixed_heads).astype(jnp.bfloat16)
    attended_f = lax.optimization_barrier(attended).astype(jnp.float32)
    mean_square = jnp.mean(attended_f * attended_f, axis=1, keepdims=True)
    normed = (attended_f * lax.rsqrt(mean_square + EPSILON) * gain_f).astype(jnp.bfloat16)
    shard_rows = lax.all_gather(normed, ("side", "grp", "shard"), axis=0, tiled=True)
    gate_proj = jnp.einsum("rd,fd->rf", shard_rows, gate_weight, preferred_element_type=jnp.float32)
    upward = jnp.einsum("rd,fd->rf", shard_rows, up_weight, preferred_element_type=jnp.float32)
    hidden = (jax.nn.silu(gate_proj) * upward).astype(jnp.bfloat16)
    terms = jnp.dot(hidden, down_weight, preferred_element_type=jnp.float32)
    summed = lax.psum_scatter(terms, ("side", "grp", "shard"), scatter_dimension=0, tiled=True)
    attended, ffn_out = (attended, summed.astype(jnp.bfloat16))
    return (attended, ffn_out)


def solution(mesh):
    placed = (
        P(("side", "grp", "shard"), None),
        P(("side", "grp", "shard"), None, None),
        P(("side", "grp", "shard"), None, None),
        P(("side", "grp", "shard"), None),
        P(("side", "grp", "shard"), None),
        P(("side", "grp", "shard")),
        P(("side", "grp", "shard"), None),
        P(),
        P(("side", "grp", "shard"), None),
        P(("side", "grp", "shard"), None),
        P(("side", "grp", "shard"), None),
    )
    return jax.shard_map(
        local,
        mesh=mesh,
        in_specs=placed,
        out_specs=(P(("side", "grp", "shard"), None), P(("side", "grp", "shard"), None)),
        check_vma=False,
    )
```

profile of v0, /device:TPU:1, one launch (start us, length us, event | category | flops | bytes accessed | tf_op | source)
XLA Modules:
  0.0 682.3 jit_solution(3482111356612227949)
XLA Ops:
  7.2 1.4 reduce_max.18
  9.3 0.8 copy.34
  10.1 0.7 reshape.107
  10.8 0.1 fusion.32
  10.9 2.2 copy_bitcast_fusion
  13.2 4.5 while.22
  13.2 0.7 broadcast_compare_fusion.4
  13.9 1.3 fusion.52
  15.2 0.2 select_reduce_fusion.2
  15.4 0.7 broadcast_compare_fusion.4
  16.2 1.3 fusion.52
  17.4 0.2 select_reduce_fusion.2
  17.7 0.7 convert_bitcast_fusion
  18.4 2.2 copy.26
  20.7 8.7 %while.23 = (s32[]{:T(128)}, f32[2,8,8,128]{3,2,1,0:T(8,128)S(1)}, s32[]{:T(128)}, s32[2]{0:T(128)}, bf16[2,192,8,128]{3,1,2,0:T(8,128)(2,1)}, /*index=5*/bf16[2...) while((s32[]{:T(128)}, f32[2,8,8,128]{3,2,1,0:T(8,128)S(1)}, ...), condition=%wide.region_6.7_spmd, body=%wide.region_5.6_spmd.sunk | while | flops 4260038 | bytes 1214783 | solution.py:67
  20.7 1.7 constant_dynamic-slice_fusion.2
  22.4 1.2 broadcast_compare_fusion.5
  23.6 1.4 convolution_add_fusion.2
  25.0 1.7 constant_dynamic-slice_fusion.2
  26.7 1.2 broadcast_compare_fusion.5
  28.0 1.4 convolution_add_fusion.2
  29.5 0.2 fusion.25
  29.7 0.7 convert_element_type.48
  30.4 0.7 fusion.29
  31.1 429.3 %all-gather.3.cloned.1.call-done = bf16[256,2,8192]{2,1,0:T(2,128)(2,1)} async-done(((bf16[1,2,8192]{2,1,0:T(2,128)(2,1)}), bf16[256,2,8192]{2,1,0:T(2,128)(2,1)}) %all-gather.3.cloned.1.call-update) | async-done | bytes 8388624 | tf_op jit(solution)/shard_map/all_gather | solution.py:90
  460.4 13.1 %reshape.103 = bf16[512,8192]{1,0:T(8,128)(2,1)} reshape(bf16[256,2,8192]{2,1,0:T(2,128)(2,1)} %all-gather.3.cloned.1.call-done) | data formatting | bytes 16777216
  473.5 7.4 %fusion.33 = f32[512,208]{0,1:T(8,128)S(1)} fusion(bf16[512,8192]{1,0:T(8,128)(2,1)} %reshape.103, bf16[208,8192]{1,0:T(8,128)(2,1)} %param.23), kind=kOutput, calls=%fused_computation.54 | convolution fusion | flops 1744830464 | bytes 12222464 | tf_op jit(solution)/shard_map/rd,fd->rf/dot_general | solution.py:91
  480.9 0.3 copy-done.4
  481.2 2.9 fusion.24
  484.1 8.1 %fusion.34 = f32[512,8192]{1,0:T(8,128)} fusion(bf16[512,208]{0,1:T(8,128)(2,1)S(1)} %fusion.24, bf16[208,8192]{1,0:T(8,128)(2,1)S(1)} %copy-done), kind=kOutput, calls=%fused_computation.55 | convolution fusion | flops 1744830464 | bytes 20398080 | tf_op jit(solution)/shard_map/dot_general | solution.py:94
  492.2 181.7 %all-reduce.2 = bf16[512,8192]{1,0:T(8,128)(2,1)} all-reduce(f32[512,8192]{1,0:T(8,128)} %fusion.34), channel_id=2, replica_groups=mesh['side'=2,'grp'=8,'shard'=16] {'side','grp','shard'}, use_global_device_ids=true, to_apply=%region_8.9.clone | all-reduce | flops 4194304 | bytes 25165824
  673.9 1.6 dynamic-slice_convert_fusion
  (28 shorter events, 0.3 us)
Async XLA Ops:
  7.2 476.9 %copy-start = (bf16[208,8192]{1,0:T(8,128)(2,1)S(1)}, bf16[208,8192]{1,0:T(8,128)(2,1)}, u32[]{:S(2)}) copy-start(bf16[208,8192]{1,0:T(8,128)(2,1)} %param.25) | copy-start | bytes 10223620
  7.2 22.2 %copy-start.3 = (bf16[2,8192]{1,0:T(2,128)(2,1)S(1)}, bf16[2,8192]{1,0:T(2,128)(2,1)}, u32[]{:S(2)}) copy-start(bf16[2,8192]{1,0:T(2,128)(2,1)} %param.21) | copy-start | bytes 98308
  7.2 453.2 %all-gather.3.cloned.1.call-start = ((), (), s32[]{:S(2)}) async-start(), calls=%async_computation | async-start | bytes 8421376 | tf_op jit(solution)/shard_map/all_gather | solution.py:90
  29.5 444.1 %copy-start.2 = (bf16[2,8192]{1,0:T(2,128)(2,1)}, bf16[2,8192]{1,0:T(2,128)(2,1)S(1)}, u32[]{:S(2)}) copy-start(bf16[2,8192]{1,0:T(2,128)(2,1)S(1)} %fusion.28) | copy-start | bytes 98308
  473.5 7.4 %copy-start.1 = (bf16[512,8192]{1,0:T(8,128)(2,1)S(1)}, bf16[512,8192]{1,0:T(8,128)(2,1)}, u32[]{:S(2)}) copy-start(bf16[512,8192]{1,0:T(8,128)(2,1)} %reshape.103) | copy-start | bytes 25165828
  473.5 7.7 %copy-start.4 = (bf16[208,8192]{1,0:T(8,128)(2,1)S(1)}, bf16[208,8192]{1,0:T(8,128)(2,1)}, u32[]{:S(2)}) copy-start(bf16[208,8192]{1,0:T(8,128)(2,1)} %param.24) | copy-start | bytes 10223620
Sparse Core Ops, SparseCore 0:
  31.3 429.1 all-gather.2
where the time goes:
time: 684 us; the launch traced here: 682 us
  waiting for transfers between devices  429 us (63%)
  blocking collectives  182 us (27%)
  local copies, waits for them, and re-layouts  24.3 us (4%)
  matrix products  23.8 us (3%)
  between operations  14.8 us (2%)
  other arithmetic  8.3 us (1%)
    all_gather x1, waiting for transfers between devices, local(): lax.all_gather(normed, ('side', 'grp', 'shard'), axis=0, tiled=True)  429 us
    unnamed x1, blocking collectives  182 us
    unnamed x14, local copies, waits for them, and re-layouts  16.4 us
  transfers between devices with their start and end apart: 1, of which 1 were waited for; matrix products, arithmetic and copies ran while one was open for 0% of the time, Pallas kernels for 0%

commit v1 on v0

v1 whole, which is shorter than its diff:
```python
import jax
import jax.numpy as jnp
from jax import lax
from jax.experimental import pallas as pl
from jax.experimental.pallas import tpu as pltpu
from jax.sharding import PartitionSpec as P

MESH = pl.DeviceIdType.MESH
F32 = jnp.float32
BF16 = jnp.bfloat16

HD = 128
KVH = 8
CACHE = 192
UNITS = 208
EPSILON = 1e-05
NEG_FILL = -1e30

RING4 = (0, 1, -1, 2)
BACK4 = (0, 2, 1, 3)
GROUPS = ((0, 1), (1, 3), (3, 5), (5, 7), (7, 8))
PLANE = 4096
PART = 2048
HALF = 1024
HALVES = (pl.ds(0, HALF), pl.ds(HALF, HALF))


def kernel(
    q_ref, resid_ref, newk_ref, newv_ref, len_ref, gain_ref,
    k_hbm, v_hbm, gate_hbm, up_hbm, down_hbm,
    att_ref, ffn_ref,
    kb, vb, wg, wu, wd, qs, rs_, at, ns, r1, xs, pa, pn, pr, haf, hab, hbb,
    tb, un, fr, cr, zs, zr, qf, ff,
    send_sems, recv_sems, local_sems,
):
    side = lax.axis_index("side")
    grp = lax.axis_index("grp")
    shard = lax.axis_index("shard")
    x = lax.rem(grp, 2) * 2 + side
    y = grp // 2
    z = shard // 2
    c = lax.rem(shard, 2)
    oc = 1 - c

    def device(dx=0, dy=0, dz=0, core=c):
        xx = lax.rem(x + dx + 4, 4)
        yy = lax.rem(y + dy + 4, 4)
        zz = lax.rem(z + dz + 8, 8)
        return (lax.rem(xx, 2), yy * 2 + xx // 2, zz * 2 + core)

    def along(part, d, core=c):
        return device(dx=d, core=core) if part == 0 else device(dy=d, core=core)

    def across(part, d, core=c):
        return along(1 - part, d, core)

    sends = []
    counts = [0, 0]

    def remote(src, dst, target):
        i = counts[0]
        counts[0] += 1
        copy = pltpu.make_async_remote_copy(
            src_ref=src, dst_ref=dst, send_sem=send_sems.at[i], recv_sem=recv_sems.at[i],
            device_id=target, device_id_type=MESH,
        )
        copy.start()
        sends.append(copy)
        return copy

    def local(src, dst):
        i = counts[1]
        counts[1] += 1
        copy = pltpu.make_async_copy(src, dst, local_sems.at[i])
        copy.start()
        return copy

    barrier = pltpu.get_barrier_semaphore()
    peers = [device(core=oc), device(dz=1), device(dz=-1)]
    for d in RING4[1:]:
        for core in (c, oc):
            peers.append(device(dx=d, core=core))
            peers.append(device(dy=d, core=core))
    for peer in peers:
        pl.semaphore_signal(barrier, inc=1, device_id=peer, device_id_type=MESH)

    cache_loads = [local(k_hbm, kb), local(v_hbm, vb)]
    mine = pl.ds(pl.multiple_of(c * UNITS, 16), UNITS)
    own_cols = pl.ds(pl.multiple_of(c * PLANE, PLANE), PLANE)
    other_cols = pl.ds(pl.multiple_of(oc * PLANE, PLANE), PLANE)
    weights = ((gate_hbm, wg), (up_hbm, wu), (down_hbm, wd))
    weight_loads = [local(h.at[:, own_cols], w.at[mine]) for h, w in weights]

    pl.semaphore_wait(barrier, len(peers))
    weight_swaps = [remote(h.at[:, other_cols], w.at[mine], device(core=oc)) for h, w in weights]

    qv = q_ref[...].astype(F32)
    rv = resid_ref[...].astype(F32)
    for j in range(64):
        qs[pl.ds(j, 2, stride=64), :] = qv[:, j * HD:(j + 1) * HD]
        rs_[pl.ds(j, 2, stride=64), :] = rv[:, j * HD:(j + 1) * HD]
    newk = newk_ref[...].astype(F32)
    newv = newv_ref[...].astype(F32)
    row = lax.broadcasted_iota(jnp.int32, (16, 2 * CACHE), 0)
    col = lax.broadcasted_iota(jnp.int32, (16, 2 * CACHE), 1)
    slot_of = jnp.where(row < 8, col, col - CACHE)
    filled = jnp.where(row < 8, len_ref[0], len_ref[1])
    valid = (slot_of >= 0) & (slot_of < filled)
    for load in cache_loads:
        load.wait()
    first = lax.broadcasted_iota(jnp.int32, (16, HD), 0) < 8

    def both(rows, k):
        one = rows[0:1, k * HD:(k + 1) * HD]
        two = rows[1:2, k * HD:(k + 1) * HD]
        return jnp.where(first, one, two)

    scale = HD ** (-0.5)
    scored = []
    for k in range(KVH):
        q16 = jnp.concatenate([qs[8 * k:8 * k + 8, :], qs[64 + 8 * k:72 + 8 * k, :]], axis=0)
        keys = kb[:, :, k * HD:(k + 1) * HD].reshape(2 * CACHE, HD)
        s = lax.dot_general(
            q16.astype(BF16), keys, (((1,), (1,)), ((), ())), preferred_element_type=F32
        ) * scale
        own = jnp.sum(q16 * both(newk, k), axis=1, keepdims=True) * scale
        scored.append((jnp.where(valid, s, NEG_FILL), own))
    weighted = []
    for s, own in scored:
        top = jnp.maximum(jnp.max(s, axis=1, keepdims=True), own)
        e = jnp.where(valid, jnp.exp(s - top), 0.0)
        own_e = jnp.exp(own - top)
        total = jnp.sum(e, axis=1, keepdims=True) + own_e
        weighted.append(((e / total).astype(BF16), (own_e / total).astype(BF16).astype(F32)))
    for k, (p, own_p) in enumerate(weighted):
        values = vb[:, :, k * HD:(k + 1) * HD].reshape(2 * CACHE, HD)
        mixed = jnp.dot(p, values, preferred_element_type=F32) + own_p * both(newv, k)
        for r in range(2):
            rows = pl.ds(r * 64 + 8 * k, 8)
            at[rows, :] = (rs_[rows, :] + mixed[8 * r:8 * r + 8]).astype(BF16).astype(F32)

    gain = gain_ref[...].astype(F32)
    for r in range(2):
        a = at[r * 64:(r + 1) * 64, :]
        mean_square = jnp.sum(a * a, keepdims=True).reshape(1, 1) * (1.0 / 8192)
        normed = (a * lax.rsqrt(mean_square + EPSILON) * gain).astype(BF16).astype(F32)
        for plane in range(2):
            for part in range(2):
                j = plane * 32 + part * 16
                ns[part, plane, r * 16:(r + 1) * 16, :] = normed[j:j + 16]

    def src_rows(slot, core):
        return pl.ds(pl.multiple_of((slot * 2 + core) * 32, 32), 32)

    first_copies = []
    for part in range(2):
        for d in (2, 1, -1):
            slot = BACK4[RING4.index(d)]
            for core in (c, oc):
                first_copies.append((part, remote(
                    ns.at[part, core], r1.at[part, src_rows(slot, c)], across(part, d, core))))
        first_copies.append((part, remote(
            ns.at[part, oc], r1.at[part, src_rows(0, c)], device(core=oc))))
        r1[part, src_rows(0, c), :] = ns[part, c]
    for j in range(64):
        att_ref[:, j * HD:(j + 1) * HD] = at[pl.ds(j, 2, stride=64), :].astype(BF16)

    z_copies = {}
    x_copies = {}
    f_copies = {}

    def z_send(part, k):
        ahead, behind = 2 * k, max(2 * k - 1, 0)
        if k < 3:
            z_copies[part, k] = (
                remote(xs.at[part, ahead, 0], xs.at[part, 2 * k + 2, 0], device(dz=1)),
                remote(xs.at[part, behind, 0], xs.at[part, 2 * k + 1, 0], device(dz=-1)),
            )
        else:
            z_copies[part, k] = tuple(
                remote(xs.at[part, s, 0, :, h], xs.at[part, 7, 0, :, h], device(dz=d))
                for s, h, d in ((ahead, HALVES[0], 1), (behind, HALVES[1], -1))
            )

    def x_send(part, g):
        zz = pl.ds(GROUPS[g][0], GROUPS[g][1] - GROUPS[g][0])
        x_copies[part, g] = (
            remote(xs.at[part, zz, 0], xs.at[part, zz, 2], along(part, 1)),
            remote(xs.at[part, zz, 0], xs.at[part, zz, 1], along(part, -1)),
        )

    def x_forward(part, g):
        zz = pl.ds(GROUPS[g][0], GROUPS[g][1] - GROUPS[g][0])
        x_copies[part, g][0].wait_recv()
        far0 = remote(xs.at[part, zz, 2, :, HALVES[0]], xs.at[part, zz, 3, :, HALVES[0]], along(part, 1))
        x_copies[part, g][1].wait_recv()
        far1 = remote(xs.at[part, zz, 1, :, HALVES[1]], xs.at[part, zz, 3, :, HALVES[1]], along(part, -1))
        f_copies[part, g] = (far0, far1)

    for part in range(2):
        for p, copy in first_copies:
            if p == part:
                copy.wait_recv()
        for j in range(16):
            xs[part, 0, 0, :, j * HD:(j + 1) * HD] = r1[part, pl.ds(j, 16, stride=16), :].astype(BF16)
        z_send(part, 0)
        x_send(part, 0)

    p_copies = {}
    far_copies = {}
    near_copies = {}

    def gates(g):
        a, b = GROUPS[g]
        n, m = b - a, 64 * (b - a)
        rows = pl.ds(a * 64, m)
        for part in range(2):
            for copy in f_copies[part, g]:
                copy.wait_recv()
        for i, w in enumerate((wg, wu)):
            dots = [
                lax.dot_general(
                    xs[part, a:b].reshape(m, PART), w[:, part * PART:(part + 1) * PART],
                    (((1,), (1,)), ((), ())), preferred_element_type=F32,
                ) for part in range(2)
            ]
            for s in range(n):
                for u in range(4):
                    for v in range(4):
                        pa[i, s * 64 + u * 16 + v * 4:s * 64 + u * 16 + v * 4 + 4, :] = (
                            dots[0][s * 64 + v * 16 + u * 4:s * 64 + v * 16 + u * 4 + 4])
            pn[i, rows, :] = pa[i, :m, :] + dots[1]
        p_copies[g] = remote(pn.at[:, rows], pr.at[:, rows], device(core=oc))

    def hidden_down(g):
        a, b = GROUPS[g]
        n, m = b - a, 64 * (b - a)
        rows = pl.ds(a * 64, m)
        p_copies[g].wait_recv()
        gate = pn[0, rows, :] + pr[0, rows, :]
        up = pn[1, rows, :] + pr[1, rows, :]
        hidden = gate / (1.0 + jnp.exp(-gate)) * up
        hbb[:m, :] = hidden.astype(BF16)
        for s in range(n):
            for u in range(4):
                for v in range(4):
                    haf[s * 64 + u * 16 + v * 4:s * 64 + u * 16 + v * 4 + 4, :] = (
                        hidden[s * 64 + v * 16 + u * 4:s * 64 + v * 16 + u * 4 + 4])
        hab[:m, :] = haf[:m, :].astype(BF16)
        zz = pl.ds(a, n)
        for part, h in enumerate((hab, hbb)):
            for t in range(4):
                cols = pl.ds(t * 512, 512)
                term = jnp.dot(
                    h[:m, :], wd[:, part * PART + t * 512:part * PART + (t + 1) * 512],
                    preferred_element_type=F32,
                ).reshape(n, 4, 16, 512)
                un[part, zz, :, cols] = term[:, 0]
                tb[part, zz, :, :, cols] = term[:, 1:].astype(BF16)
            far_copies[part, g] = tuple(
                remote(tb.at[part, zz, 2, :, HALVES[i]], fr.at[part, i, zz], along(part, d))
                for i, d in enumerate((1, -1))
            )

    def relay(g):
        zz = pl.ds(GROUPS[g][0], GROUPS[g][1] - GROUPS[g][0])
        for part in range(2):
            copies = []
            for i, d in enumerate((1, -1)):
                far_copies[part, g][i].wait_recv()
                near = tb[part, zz, i, :, HALVES[i]].astype(F32) + fr[part, i, zz].astype(F32)
                tb[part, zz, i, :, HALVES[i]] = near.astype(BF16)
                copies.append(remote(tb.at[part, zz, i], cr.at[part, i, zz], along(part, d)))
            near_copies[part, g] = copies

    def collect(g):
        zz = pl.ds(GROUPS[g][0], GROUPS[g][1] - GROUPS[g][0])
        for part in range(2):
            for copy in near_copies[part, g]:
                copy.wait_recv()
            un[part, zz] = un[part, zz] + (cr[part, 0, zz].astype(F32) + cr[part, 1, zz].astype(F32))

    def z_step(k):
        for part in range(2):
            for copy in z_copies[part, k - 1]:
                copy.wait_recv()
            if k < 4:
                z_send(part, k)
            x_send(part, k)

    def forward(g):
        for part in range(2):
            x_forward(part, g)

    z_step(1)
    forward(0)
    z_step(2)
    forward(1)
    for copy in weight_loads:
        copy.wait()
    for copy in weight_swaps:
        copy.wait_recv()
    gates(0)
    z_step(3)
    forward(2)
    gates(1)
    hidden_down(0)
    z_step(4)
    forward(3)
    gates(2)
    hidden_down(1)
    relay(0)
    forward(4)
    gates(3)
    hidden_down(2)
    relay(1)
    collect(0)
    gates(4)
    hidden_down(3)
    relay(2)
    collect(1)
    hidden_down(4)
    relay(3)
    collect(2)
    relay(4)
    collect(3)
    collect(4)

    zc = {}
    for step in range(5):
        for part in range(2):
            if step > 0:
                for copy in zc[part, step - 1]:
                    copy.wait_recv()
            if step == 4:
                un[part, 0] = un[part, 0] + (zr[part, 0, 3].astype(F32) + zr[part, 1, 3].astype(F32))
                continue
            copies = []
            for i, d in enumerate((1, -1)):
                if step == 0:
                    zs[part, i, 0, :, HALVES[i]] = un[part, 7, :, HALVES[i]].astype(BF16)
                    copies.append(remote(
                        zs.at[part, i, 0, :, HALVES[i]], zr.at[part, i, 0, :, HALVES[i]], device(dz=d)))
                    continue
                block = 2 * (4 - step) - 1 + i
                if step == 1:
                    zs[part, i, 1, :, HALVES[1 - i]] = un[part, block, :, HALVES[1 - i]].astype(BF16)
                    zs[part, i, 1, :, HALVES[i]] = (
                        un[part, block, :, HALVES[i]] + zr[part, i, 0, :, HALVES[i]].astype(F32)).astype(BF16)
                else:
                    zs[part, i, step] = (un[part, block] + zr[part, i, step - 1].astype(F32)).astype(BF16)
                copies.append(remote(zs.at[part, i, step], zr.at[part, i, step], device(dz=d)))
            zc[part, step] = copies

    last_copies = []
    for part in range(2):
        for j in range(16):
            qf[part, pl.ds(j, 16, stride=16), :] = un[part, 0, :, j * HD:(j + 1) * HD]
        for s, d in ((3, 2), (1, 1), (2, -1)):
            for core in (c, oc):
                last_copies.append(remote(
                    qf.at[part, src_rows(s, core)], ff.at[part, c, BACK4[s]], across(part, d, core)))
        last_copies.append(remote(qf.at[part, src_rows(0, oc)], ff.at[part, c, 0], device(core=oc)))
        ff[part, c, 0] = qf[part, src_rows(0, c), :]
    for copy in last_copies:
        copy.wait_recv()
    for plane in range(2):
        for part in range(2):
            total = (ff[part, plane, 0] + ff[part, plane, 1]) + (ff[part, plane, 2] + ff[part, plane, 3])
            qs[0:32, :] = total
            for j in range(16):
                first_col = (plane * 32 + part * 16 + j) * HD
                ffn_ref[:, first_col:first_col + HD] = qs[pl.ds(j, 2, stride=16), :].astype(BF16)
    for copy in sends:
        copy.wait_send()


N_REMOTE = 3 + 14 + 16 + 20 + 20 + 5 + 20 + 20 + 16 + 14


def local(
    queries, key_cache, value_cache, new_keys, new_values, lengths, resid_in, norm_gain,
    gate_weight, up_weight, down_weight,
):
    vmem = pl.BlockSpec(memory_space=pltpu.VMEM)
    smem = pl.BlockSpec(memory_space=pltpu.SMEM)
    hbm = pl.BlockSpec(memory_space=pl.ANY)
    out = jax.ShapeDtypeStruct((2, 8192), BF16)
    return pl.pallas_call(
        kernel,
        out_shape=(out, out),
        in_specs=[vmem, vmem, vmem, vmem, smem, vmem] + [hbm] * 5,
        out_specs=(vmem, vmem),
        scratch_shapes=[
            pltpu.VMEM((2, CACHE, 1024), BF16),
            pltpu.VMEM((2, CACHE, 1024), BF16),
            pltpu.VMEM((2 * UNITS, PLANE), BF16),
            pltpu.VMEM((2 * UNITS, PLANE), BF16),
            pltpu.VMEM((2 * UNITS, PLANE), BF16),
            pltpu.VMEM((128, 128), F32),
            pltpu.VMEM((128, 128), F32),
            pltpu.VMEM((128, 128), F32),
            pltpu.VMEM((2, 2, 32, 128), F32),
            pltpu.VMEM((2, 256, 128), F32),
            pltpu.VMEM((2, 8, 4, 16, PART), BF16),
            pltpu.VMEM((2, 128, 2 * UNITS), F32),
            pltpu.VMEM((2, 512, 2 * UNITS), F32),
            pltpu.VMEM((2, 512, 2 * UNITS), F32),
            pltpu.VMEM((128, 2 * UNITS), F32),
            pltpu.VMEM((128, 2 * UNITS), BF16),
            pltpu.VMEM((128, 2 * UNITS), BF16),
            pltpu.VMEM((2, 8, 3, 16, PART), BF16),
            pltpu.VMEM((2, 8, 16, PART), F32),
            pltpu.VMEM((2, 2, 8, 16, HALF), BF16),
            pltpu.VMEM((2, 2, 8, 16, PART), BF16),
            pltpu.VMEM((2, 2, 4, 16, PART), BF16),
            pltpu.VMEM((2, 2, 4, 16, PART), BF16),
            pltpu.VMEM((2, 256, 128), F32),
            pltpu.VMEM((2, 2, 4, 32, 128), F32),
            pltpu.SemaphoreType.DMA((N_REMOTE,)),
            pltpu.SemaphoreType.DMA((N_REMOTE,)),
            pltpu.SemaphoreType.DMA((5,)),
        ],
        compiler_params=pltpu.CompilerParams(
            collective_id=0, has_side_effects=True, vmem_limit_bytes=56 * 2**20
        ),
        name="decode_layer",
    )(
        queries, resid_in, new_keys, new_values, lengths, norm_gain.reshape(64, 128),
        key_cache, value_cache, gate_weight, up_weight, down_weight,
    )


def solution(mesh):
    rows = P(("side", "grp", "shard"), None)
    cache = P(("side", "grp", "shard"), None, None)
    return jax.shard_map(
        local,
        mesh=mesh,
        in_specs=(rows, cache, cache, rows, rows, P(("side", "grp", "shard")), rows, P(), rows, rows, rows),
        out_specs=(rows, rows),
        check_vma=False,
    )
```

time: 684 us -> 86.9 us (0.13)
  waiting for transfers between devices: 429 us -> 0 us
  blocking collectives: 182 us -> 0 us
  Pallas kernels: 0 us -> 83.2 us
  matrix products: 23.8 us -> 0 us
  local copies, waits for them, and re-layouts: 24.3 us -> 2.79 us
  between operations: 14.8 us -> 0.64 us
  other arithmetic: 8.3 us -> 0 us
    all_gather x1 -> x0, waiting for transfers between devices: 429 us -> none  [local(): lax.all_gather(normed, ('side', 'grp', 'shard'), axis=0, tiled=True)]
    unnamed x1 -> x0, blocking collectives: 182 us -> none
    pallas_call x0 -> x1, Pallas kernels: none -> 83.2 us  [local(): pl.pallas_call(kernel, out_shape=(out, out), in_specs=[vmem, vmem, vmem,...]
    dot_general x8 -> x0, matrix products: 23.8 us -> none  [the longest x1 8.1 us: local(): terms = jnp.dot(hidden, down_weight, preferred_element_type=jnp.float32)]
    unnamed x14 -> x2, local copies, waits for them, and re-layouts: 16.4 us -> 2.79 us
  transfers between devices with their start and end apart: 1 -> 0, of which waited for: 1 -> 0; matrix products, arithmetic and copies ran while one was open for 0% -> 0% of each run, Pallas kernels for 0% -> 0%
where the time goes in v1:
time: 86.9 us; the launch traced here: 86.7 us
  Pallas kernels  83.2 us (96%)
  local copies, waits for them, and re-layouts  2.79 us (3%)
    pallas_call x1, Pallas kernels, local(): pl.pallas_call(kernel, out_shape=(out, out), in_specs=[vmem, vmem, vmem,...  83.2 us
    unnamed x2, local copies, waits for them, and re-layouts  2.79 us

profile of v1, /device:TPU:1, one launch (start us, length us, event | category | flops | bytes accessed | tf_op | source)
XLA Modules:
  0.0 86.7 jit_solution(3098163105003654575)
XLA Ops:
  0.6 83.2 %decode_layer.1 = (bf16[2,8192]{1,0:T(2,128)(2,1)}, bf16[2,8192]{1,0:T(2,128)(2,1)}) custom-call(bf16[2,8192]{1,0:T(2,128)(2,1)} %q_ref.1, bf16[2,8192]{1,0:T(2,128)(2,1)} %resid_ref.1, bf16[2,1024]{1,0:T(2,128)(2,1)} %newk_ref.1, bf16[2,1024]{1,0:T(2,128)(2,1)} %newv_ref.1, s32[2]{0:T(128)} %len_ref.1, bf16[64,128]{1,0:T(8,128)(2,1)} %bitcast.1, ...), custom_call_target="tpu_custom_call" | custom-call | tf_op jit(solution)/shard_map/decode_layer/pallas_call | solution.py:389
  83.9 1.4 %copy.15 = bf16[2,8192]{1,0:T(2,128)(2,1)} copy(bf16[2,8192]{1,0:T(2,128)(2,1)} %get-tuple-element.4) | data formatting | bytes 65536
  85.3 1.4 %copy.16 = bf16[2,8192]{1,0:T(2,128)(2,1)} copy(bf16[2,8192]{1,0:T(2,128)(2,1)} %get-tuple-element.5) | data formatting | bytes 65536

commit v2 on v1

v2 whole, which is shorter than its diff:
```python
import jax
import jax.numpy as jnp
from jax import lax
from jax.experimental import pallas as pl
from jax.experimental.pallas import tpu as pltpu
from jax.sharding import PartitionSpec as P

MESH = pl.DeviceIdType.MESH
F32 = jnp.float32
BF16 = jnp.bfloat16

HD = 128
KVH = 8
CACHE = 192
UNITS = 208
EPSILON = 1e-05
NEG_FILL = -1e30

RING4 = (0, 1, -1, 2)
BACK4 = (0, 2, 1, 3)
GROUPS = ((0, 1), (1, 3), (3, 5), (5, 7), (7, 8))
DOTS = ((0, 1), (2,), (3, 4))
RUNS = ((0, 3), (3, 5), (5, 8))
BACKS = ((0, 3), (3, 5), (7, 8), (5, 7))
PLANE = 4096
PART = 2048
HALF = 1024
HALVES = (pl.ds(0, HALF), pl.ds(HALF, HALF))


def kernel(
    q_ref, resid_ref, newk_ref, newv_ref, len_ref, gain_ref,
    k_hbm, v_hbm, gate_hbm, up_hbm, down_hbm,
    out_ref,
    kb, vb, wg, wu, wd, qs, rs_, at, ns, r1, ex, xs, pa, pn, pr, haf, hab, hbb,
    tb, un, fr, cr, zs, zr, qf, ff,
    send_sems, recv_sems, local_sems,
):
    side = lax.axis_index("side")
    grp = lax.axis_index("grp")
    shard = lax.axis_index("shard")
    x = lax.rem(grp, 2) * 2 + side
    y = grp // 2
    z = shard // 2
    c = lax.rem(shard, 2)
    oc = 1 - c

    def device(dx=0, dy=0, dz=0, core=c):
        xx = lax.rem(x + dx + 4, 4)
        yy = lax.rem(y + dy + 4, 4)
        zz = lax.rem(z + dz + 8, 8)
        return (lax.rem(xx, 2), yy * 2 + xx // 2, zz * 2 + core)

    def along(part, d, core=c):
        return device(dx=d, core=core) if part == 0 else device(dy=d, core=core)

    def across(part, d, core=c):
        return along(1 - part, d, core)

    send_ids = {}
    recv_ids = {}

    def remote(src, dst, target, sent, got):
        i = send_ids.setdefault(sent, len(send_ids))
        j = recv_ids.setdefault(got, len(recv_ids))
        pltpu.make_async_remote_copy(
            src_ref=src, dst_ref=dst, send_sem=send_sems.at[i], recv_sem=recv_sems.at[j],
            device_id=target, device_id_type=MESH,
        ).start()

    def wait_sent(sent, ref):
        pltpu.make_async_copy(ref, ref, send_sems.at[send_ids[sent]]).wait()

    def wait_got(got, ref):
        pltpu.make_async_copy(ref, ref, recv_sems.at[recv_ids[got]]).wait()

    loads = []

    def local(src, dst):
        i = len(loads)
        loads.append(i)
        copy = pltpu.make_async_copy(src, dst, local_sems.at[i])
        copy.start()
        return copy

    barrier = pltpu.get_barrier_semaphore()
    peers = [device(core=oc), device(dz=1), device(dz=-1)]
    for d in RING4[1:]:
        for core in (c, oc):
            peers.append(device(dx=d, core=core))
            peers.append(device(dy=d, core=core))
    for peer in peers:
        pl.semaphore_signal(barrier, inc=1, device_id=peer, device_id_type=MESH)

    cache_loads = [local(k_hbm, kb), local(v_hbm, vb)]
    mine = pl.ds(pl.multiple_of(c * UNITS, 16), UNITS)
    own_cols = pl.ds(pl.multiple_of(c * PLANE, PLANE), PLANE)
    other_cols = pl.ds(pl.multiple_of(oc * PLANE, PLANE), PLANE)
    weights = ((gate_hbm, wg), (up_hbm, wu), (down_hbm, wd))
    weight_loads = [local(h.at[:, own_cols], w.at[mine]) for h, w in weights]

    qv = q_ref[...].astype(F32)
    rv = resid_ref[...].astype(F32)
    for j in range(64):
        qs[pl.ds(j, 2, stride=64), :] = qv[:, j * HD:(j + 1) * HD]
        rs_[pl.ds(j, 2, stride=64), :] = rv[:, j * HD:(j + 1) * HD]
    newk = newk_ref[...].astype(F32)
    newv = newv_ref[...].astype(F32)
    row = lax.broadcasted_iota(jnp.int32, (16, 2 * CACHE), 0)
    col = lax.broadcasted_iota(jnp.int32, (16, 2 * CACHE), 1)
    slot_of = jnp.where(row < 8, col, col - CACHE)
    filled = jnp.where(row < 8, len_ref[0], len_ref[1])
    valid = (slot_of >= 0) & (slot_of < filled)
    for load in cache_loads:
        load.wait()
    first = lax.broadcasted_iota(jnp.int32, (16, HD), 0) < 8

    def both(rows, k):
        one = rows[0:1, k * HD:(k + 1) * HD]
        two = rows[1:2, k * HD:(k + 1) * HD]
        return jnp.where(first, one, two)

    scale = HD ** (-0.5)
    scored = []
    for k in range(KVH):
        q16 = jnp.concatenate([qs[8 * k:8 * k + 8, :], qs[64 + 8 * k:72 + 8 * k, :]], axis=0)
        keys = kb[:, :, k * HD:(k + 1) * HD].reshape(2 * CACHE, HD)
        s = lax.dot_general(
            q16.astype(BF16), keys, (((1,), (1,)), ((), ())), preferred_element_type=F32
        ) * scale
        own = jnp.sum(q16 * both(newk, k), axis=1, keepdims=True) * scale
        scored.append((jnp.where(valid, s, NEG_FILL), own))
    weighted = []
    for s, own in scored:
        top = jnp.maximum(jnp.max(s, axis=1, keepdims=True), own)
        e = jnp.where(valid, jnp.exp(s - top), 0.0)
        own_e = jnp.exp(own - top)
        total = jnp.sum(e, axis=1, keepdims=True) + own_e
        weighted.append(((e / total).astype(BF16), (own_e / total).astype(BF16).astype(F32)))
    for k, (p, own_p) in enumerate(weighted):
        values = vb[:, :, k * HD:(k + 1) * HD].reshape(2 * CACHE, HD)
        mixed = jnp.dot(p, values, preferred_element_type=F32) + own_p * both(newv, k)
        for r in range(2):
            rows = pl.ds(r * 64 + 8 * k, 8)
            at[rows, :] = (rs_[rows, :] + mixed[8 * r:8 * r + 8]).astype(BF16).astype(F32)

    gain = gain_ref[...].astype(F32)
    for r in range(2):
        a = at[r * 64:(r + 1) * 64, :]
        mean_square = jnp.sum(a * a, keepdims=True).reshape(1, 1) * (1.0 / 8192)
        normed = (a * lax.rsqrt(mean_square + EPSILON) * gain).astype(BF16)
        for plane in range(2):
            for part in range(2):
                j = plane * 32 + part * 16
                ns[part, plane, r * 16:(r + 1) * 16, :] = normed[j:j + 16]

    pl.semaphore_wait(barrier, len(peers))

    def src_rows(slot, core):
        return pl.ds(pl.multiple_of((slot * 2 + core) * 32, 32), 32)

    for part in range(2):
        for d in (2, 1, -1):
            slot = BACK4[RING4.index(d)]
            for core in (c, oc):
                remote(ns.at[part, core], r1.at[part, src_rows(slot, c)], across(part, d, core), "first", ("first", part))
        remote(ns.at[part, oc], r1.at[part, src_rows(0, c)], device(core=oc), "first", ("first", part))
        r1[part, src_rows(0, c), :] = ns[part, c]
    for i, (h, w) in enumerate(weights):
        remote(h.at[:, other_cols], w.at[mine], device(core=oc), ("weight", i), ("weight", i))
    for j in range(64):
        out_ref[0:2, j * HD:(j + 1) * HD] = at[pl.ds(j, 2, stride=64), :].astype(BF16)

    def z_send(part, k):
        ahead, behind = 2 * k, max(2 * k - 1, 0)
        sent, got = "z", ("z", part, k)
        if k < 3:
            remote(xs.at[part, ahead, 0], xs.at[part, 2 * k + 2, 0], device(dz=1), sent, got)
            remote(xs.at[part, behind, 0], xs.at[part, 2 * k + 1, 0], device(dz=-1), sent, got)
        else:
            for s, h, d in ((ahead, HALVES[0], 1), (behind, HALVES[1], -1)):
                remote(xs.at[part, s, 0, :, h], xs.at[part, 7, 0, :, h], device(dz=d), sent, got)

    def z_wait(part, k):
        wait_got(("z", part, k), xs.at[part, 2 * k + 1:2 * k + 3, 0] if k < 3 else xs.at[part, 7, 0])

    def x_send(part, g):
        zz = pl.ds(GROUPS[g][0], GROUPS[g][1] - GROUPS[g][0])
        remote(xs.at[part, zz, 0], xs.at[part, zz, 2], along(part, 1), "x", ("x", part, g))
        remote(xs.at[part, zz, 0], xs.at[part, zz, 1], along(part, -1), "x", ("x", part, g))

    def x_forward(part, g):
        zz = pl.ds(GROUPS[g][0], GROUPS[g][1] - GROUPS[g][0])
        wait_got(("x", part, g), xs.at[part, zz, 1:3])
        for s, h, d in ((2, HALVES[0], 1), (1, HALVES[1], -1)):
            remote(xs.at[part, zz, s, :, h], xs.at[part, zz, 3, :, h], along(part, d), "x", ("far", part, g))

    for part in range(2):
        wait_got(("first", part), r1.at[part, 0:224])
        ex[...] = r1[part].astype(F32)
        for j in range(16):
            xs[part, 0, 0, :, j * HD:(j + 1) * HD] = ex[pl.ds(j, 16, stride=16), :].astype(BF16)
        z_send(part, 0)
        x_send(part, 0)

    def gates(g, i):
        a, b = RUNS[g]
        n, m = b - a, 64 * (b - a)
        rows = pl.ds(a * 64, m)
        if i == 0:
            for part in range(2):
                for one in DOTS[g]:
                    wait_got(("far", part, one), xs.at[part, GROUPS[one][0]:GROUPS[one][1], 3])
        dots = [
            lax.dot_general(
                xs[part, a:b].reshape(m, PART), (wg, wu)[i][:, part * PART:(part + 1) * PART],
                (((1,), (1,)), ((), ())), preferred_element_type=F32,
            ) for part in range(2)
        ]
        for s in range(n):
            for u in range(4):
                for v in range(4):
                    pa[i, s * 64 + u * 16 + v * 4:s * 64 + u * 16 + v * 4 + 4, :] = (
                        dots[0][s * 64 + v * 16 + u * 4:s * 64 + v * 16 + u * 4 + 4])
        pn[i, rows, :] = pa[i, :m, :] + dots[1]
        remote(pn.at[i, rows], pr.at[i, rows], device(core=oc), "dots", ("dots", i, g))

    def hidden_down(g):
        a, b = RUNS[g]
        n, m = b - a, 64 * (b - a)
        rows = pl.ds(a * 64, m)
        wait_got(("dots", 0, g), pr.at[0, rows])
        gate = pn[0, rows, :] + pr[0, rows, :]
        wait_got(("dots", 1, g), pr.at[1, rows])
        up = pn[1, rows, :] + pr[1, rows, :]
        hidden = gate / (1.0 + jnp.exp(-gate)) * up
        hbb[:m, :] = hidden.astype(BF16)
        for s in range(n):
            for u in range(4):
                for v in range(4):
                    haf[s * 64 + u * 16 + v * 4:s * 64 + u * 16 + v * 4 + 4, :] = (
                        hidden[s * 64 + v * 16 + u * 4:s * 64 + v * 16 + u * 4 + 4])
        hab[:m, :] = haf[:m, :].astype(BF16)
        zz = pl.ds(a, n)
        for part, h in enumerate((hab, hbb)):
            for t in range(4):
                cols = pl.ds(t * 512, 512)
                term = jnp.dot(
                    h[:m, :], wd[:, part * PART + t * 512:part * PART + (t + 1) * 512],
                    preferred_element_type=F32,
                ).reshape(n, 4, 16, 512)
                un[part, zz, :, cols] = term[:, 0]
                tb[part, zz, :, :, cols] = term[:, 1:].astype(BF16)

    def depart(g):
        zz = pl.ds(BACKS[g][0], BACKS[g][1] - BACKS[g][0])
        for part in range(2):
            for i, d in enumerate((1, -1)):
                remote(tb.at[part, zz, 2, :, HALVES[i]], fr.at[part, i, zz], along(part, d), "sum", ("relay", part, g))
        for part in range(2):
            for i, d in enumerate((1, -1)):
                h = HALVES[1 - i]
                remote(tb.at[part, zz, i, :, h], cr.at[part, i, zz, :, h], along(part, d), "sum", ("near", part, g))

    def relay(g):
        zz = pl.ds(BACKS[g][0], BACKS[g][1] - BACKS[g][0])
        for part in range(2):
            wait_got(("relay", part, g), fr.at[part, :, zz])
            for i, d in enumerate((1, -1)):
                h = HALVES[i]
                near = tb[part, zz, i, :, h].astype(F32) + fr[part, i, zz].astype(F32)
                tb[part, zz, i, :, h] = near.astype(BF16)
                remote(tb.at[part, zz, i, :, h], cr.at[part, i, zz, :, h], along(part, d), "sum", ("near", part, g))

    def collect(g):
        zz = pl.ds(BACKS[g][0], BACKS[g][1] - BACKS[g][0])
        for part in range(2):
            wait_got(("near", part, g), cr.at[part, :, zz])
            un[part, zz] = un[part, zz] + (cr[part, 0, zz].astype(F32) + cr[part, 1, zz].astype(F32))

    def z_step(k):
        for part in range(2):
            z_wait(part, k - 1)
            if k < 4:
                z_send(part, k)
            x_send(part, k)

    def forward(g):
        for part in range(2):
            x_forward(part, g)

    def z_sum(step):
        for h in range(2):
            for part in range(2):
                hh = HALVES[h]
                if step > 0:
                    got = ("zsum", part, h, step - 1)
                    wait_got(got, zr.at[part, 0, 0, :, hh] if step == 1 else zr.at[part, :, step - 1, :, hh])
                if step == 4:
                    un[part, 0, :, hh] = un[part, 0, :, hh] + (
                        zr[part, 0, 3, :, hh].astype(F32) + zr[part, 1, 3, :, hh].astype(F32))
                    continue
                for i, d in enumerate((1, -1)):
                    if step == 0 and i != h:
                        continue
                    total = un[part, 7 if step == 0 else 2 * (4 - step) - 1 + i, :, hh]
                    if step > 1 or (step == 1 and i == h):
                        total = total + zr[part, i, step - 1, :, hh].astype(F32)
                    zs[part, i, step, :, hh] = total.astype(BF16)
                    remote(zs.at[part, i, step, :, hh], zr.at[part, i, step, :, hh], device(dz=d),
                           "zsum", ("zsum", part, h, step))

    z_step(1)
    forward(0)
    z_step(2)
    forward(1)
    z_step(3)
    forward(2)
    for copy in weight_loads:
        copy.wait()
    for i, (h, w) in enumerate(weights):
        wait_got(("weight", i), w.at[mine])
    gates(0, 0)
    z_step(4)
    gates(0, 1)
    forward(3)
    gates(1, 0)
    forward(4)
    gates(1, 1)
    hidden_down(0)
    depart(0)
    gates(2, 0)
    gates(2, 1)
    hidden_down(1)
    relay(0)
    hidden_down(2)
    depart(2)
    depart(3)
    collect(0)
    relay(2)
    relay(3)
    depart(1)
    collect(2)
    z_sum(0)
    collect(3)
    z_sum(1)
    relay(1)
    collect(1)
    z_sum(2)
    z_sum(3)
    z_sum(4)

    for part in range(2):
        for j in range(16):
            ex[pl.ds(j, 16, stride=16), :] = un[part, 0, :, j * HD:(j + 1) * HD]
        qf[part] = ex[...].astype(BF16)
        for s, d in ((3, 2), (1, 1), (2, -1)):
            for core in (c, oc):
                remote(qf.at[part, src_rows(s, core)], ff.at[part, c, BACK4[s]], across(part, d, core), "last", "last")
        remote(qf.at[part, src_rows(0, oc)], ff.at[part, c, 0], device(core=oc), "last", "last")
        ff[part, c, 0] = qf[part, src_rows(0, c), :]
    for sent, ref in (
        ("first", r1.at[:, 0:224]), ("z", xs.at[:, 0:7, 0]), ("x", xs.at[:, :, 0:3]), ("dots", pn),
        ("sum", tb), ("zsum", xs.at[:, 0:7, 0]),
    ):
        wait_sent(sent, ref)
    for i, (h, w) in enumerate(weights):
        wait_sent(("weight", i), w.at[mine])
    wait_got("last", qf.at[:, 0:224])
    for plane in range(2):
        for part in range(2):
            four = [ff[part, plane, i].astype(F32) for i in range(4)]
            total = (four[0] + four[1]) + (four[2] + four[3])
            qs[0:32, :] = total
            for j in range(16):
                first_col = (plane * 32 + part * 16 + j) * HD
                out_ref[2:4, first_col:first_col + HD] = qs[pl.ds(j, 2, stride=16), :].astype(BF16)
    wait_sent("last", qf.at[:, 0:224])
    assert len(send_ids) <= N_SEND and len(recv_ids) <= N_RECV, (len(send_ids), len(recv_ids))


N_SEND = 10
N_RECV = 72


def local(
    queries, key_cache, value_cache, new_keys, new_values, lengths, resid_in, norm_gain,
    gate_weight, up_weight, down_weight,
):
    vmem = pl.BlockSpec(memory_space=pltpu.VMEM)
    smem = pl.BlockSpec(memory_space=pltpu.SMEM)
    hbm = pl.BlockSpec(memory_space=pl.ANY)
    both = pl.pallas_call(
        kernel,
        out_shape=jax.ShapeDtypeStruct((4, 8192), BF16),
        in_specs=[vmem, vmem, vmem, vmem, smem, vmem] + [hbm] * 5,
        out_specs=vmem,
        scratch_shapes=[
            pltpu.VMEM((2, CACHE, 1024), BF16),
            pltpu.VMEM((2, CACHE, 1024), BF16),
            pltpu.VMEM((2 * UNITS, PLANE), BF16),
            pltpu.VMEM((2 * UNITS, PLANE), BF16),
            pltpu.VMEM((2 * UNITS, PLANE), BF16),
            pltpu.VMEM((128, 128), F32),
            pltpu.VMEM((128, 128), F32),
            pltpu.VMEM((128, 128), F32),
            pltpu.VMEM((2, 2, 32, 128), BF16),
            pltpu.VMEM((2, 256, 128), BF16),
            pltpu.VMEM((256, 128), F32),
            pltpu.VMEM((2, 8, 4, 16, PART), BF16),
            pltpu.VMEM((2, 192, 2 * UNITS), F32),
            pltpu.VMEM((2, 512, 2 * UNITS), F32),
            pltpu.VMEM((2, 512, 2 * UNITS), F32),
            pltpu.VMEM((192, 2 * UNITS), F32),
            pltpu.VMEM((192, 2 * UNITS), BF16),
            pltpu.VMEM((192, 2 * UNITS), BF16),
            pltpu.VMEM((2, 8, 3, 16, PART), BF16),
            pltpu.VMEM((2, 8, 16, PART), F32),
            pltpu.VMEM((2, 2, 8, 16, HALF), BF16),
            pltpu.VMEM((2, 2, 8, 16, PART), BF16),
            pltpu.VMEM((2, 2, 4, 16, PART), BF16),
            pltpu.VMEM((2, 2, 4, 16, PART), BF16),
            pltpu.VMEM((2, 256, 128), BF16),
            pltpu.VMEM((2, 2, 4, 32, 128), BF16),
            pltpu.SemaphoreType.DMA((N_SEND,)),
            pltpu.SemaphoreType.DMA((N_RECV,)),
            pltpu.SemaphoreType.DMA((5,)),
        ],
        compiler_params=pltpu.CompilerParams(
            collective_id=0, has_side_effects=True, vmem_limit_bytes=56 * 2**20
        ),
        name="decode_layer",
    )(
        queries, resid_in, new_keys, new_values, lengths, norm_gain.reshape(64, 128),
        key_cache, value_cache, gate_weight, up_weight, down_weight,
    )
    return both[:2], both[2:]


def solution(mesh):
    rows = P(("side", "grp", "shard"), None)
    cache = P(("side", "grp", "shard"), None, None)
    return jax.shard_map(
        local,
        mesh=mesh,
        in_specs=(rows, cache, cache, rows, rows, P(("side", "grp", "shard")), rows, P(), rows, rows, rows),
        out_specs=(rows, rows),
        check_vma=False,
    )
```

time: 86.9 us -> 78.4 us (0.902)
  Pallas kernels: 83.2 us -> 76 us
  local copies, waits for them, and re-layouts: 2.79 us -> 1.6 us
    pallas_call x1, Pallas kernels: 83.2 us -> 76 us  [local(): pl.pallas_call(kernel, out_shape=jax.ShapeDtypeStruct((4, 8192), BF16), i...]
    unnamed x2 -> x0, local copies, waits for them, and re-layouts: 2.79 us -> none
    slice x0 -> x1, local copies, waits for them, and re-layouts: none -> 1.6 us  [local(): return (both[:2], both[2:])]
where the time goes in v2:
time: 78.4 us; the launch traced here: 78.2 us
  Pallas kernels  76 us (97%)
  local copies, waits for them, and re-layouts  1.6 us (2%)
    pallas_call x1, Pallas kernels, local(): pl.pallas_call(kernel, out_shape=jax.ShapeDtypeStruct((4, 8192), BF16), i...  76 us
    slice x1, local copies, waits for them, and re-layouts, local(): return (both[:2], both[2:])  1.6 us

profile of v2, /device:TPU:1, one launch (start us, length us, event | category | flops | bytes accessed | tf_op | source)
XLA Modules:
  0.0 78.2 jit_solution(9857166554731093492)
XLA Ops:
  0.6 76.0 %decode_layer.1 = bf16[4,8192]{1,0:T(4,128)(2,1)} custom-call(bf16[2,8192]{1,0:T(2,128)(2,1)} %q_ref.1, bf16[2,8192]{1,0:T(2,128)(2,1)} %resid_ref.1, bf16[2,1024]{1,0:T(2,128)(2,1)} %newk_ref.1, bf16[2,1024]{1,0:T(2,128)(2,1)} %newv_ref.1, s32[2]{0:T(128)} %len_ref.1, bf16[64,128]{1,0:T(8,128)(2,1)} %bitcast.1, bf16[2,192,1024]{2,1,0:T(8,128)(2,1)} %k_hbm.1, ...), custom_call_target="tpu_custom_call" | custom-call | tf_op jit(solution)/shard_map/decode_layer/pallas_call | solution.py:393
  76.6 1.6 %fusion = (bf16[2,8192]{1,0:T(2,128)(2,1)}, bf16[2,8192]{1,0:T(2,128)(2,1)}) fusion(bf16[4,8192]{1,0:T(4,128)(2,1)} %decode_layer.1), kind=kLoop, calls=%fused_computation | loop fusion | bytes 131072 | tf_op jit(solution)/shard_map/slice | solution.py:437

commit v3 on v2

--- a/solution.py
+++ b/solution.py
@@ -29,10 +29,10 @@
 
 
 def kernel(
-    q_ref, resid_ref, newk_ref, newv_ref, len_ref, gain_ref,
+    q_hbm, resid_hbm, newk_hbm, newv_hbm, len_ref, gain_hbm,
     k_hbm, v_hbm, gate_hbm, up_hbm, down_hbm,
     out_ref,
-    kb, vb, wg, wu, wd, qs, rs_, at, ns, r1, ex, xs, pa, pn, pr, haf, hab, hbb,
+    q_ref, resid_ref, newk_ref, newv_ref, gain_ref, kb, vb, wg, wu, wd, qs, rs_, at, ns, r1, ex, xs, pa, pn, pr, haf, hab, hbb,
     tb, un, fr, cr, zs, zr, qf, ff,
     send_sems, recv_sems, local_sems,
 ):
@@ -83,6 +83,10 @@
         copy.start()
         return copy
 
+    row_loads = [local(h, w) for h, w in (
+        (q_hbm, q_ref), (resid_hbm, resid_ref), (newk_hbm, newk_ref), (newv_hbm, newv_ref), (gain_hbm, gain_ref))]
+    cache_loads = [local(k_hbm, kb), local(v_hbm, vb)]
+
     barrier = pltpu.get_barrier_semaphore()
     peers = [device(core=oc), device(dz=1), device(dz=-1)]
     for d in RING4[1:]:
@@ -92,13 +96,14 @@
     for peer in peers:
         pl.semaphore_signal(barrier, inc=1, device_id=peer, device_id_type=MESH)
 
-    cache_loads = [local(k_hbm, kb), local(v_hbm, vb)]
     mine = pl.ds(pl.multiple_of(c * UNITS, 16), UNITS)
     own_cols = pl.ds(pl.multiple_of(c * PLANE, PLANE), PLANE)
     other_cols = pl.ds(pl.multiple_of(oc * PLANE, PLANE), PLANE)
     weights = ((gate_hbm, wg), (up_hbm, wu), (down_hbm, wd))
     weight_loads = [local(h.at[:, own_cols], w.at[mine]) for h, w in weights]
 
+    for load in row_loads:
+        load.wait()
     qv = q_ref[...].astype(F32)
     rv = resid_ref[...].astype(F32)
     for j in range(64):
@@ -171,18 +176,18 @@
     for j in range(64):
         out_ref[0:2, j * HD:(j + 1) * HD] = at[pl.ds(j, 2, stride=64), :].astype(BF16)
 
-    def z_send(part, k):
-        ahead, behind = 2 * k, max(2 * k - 1, 0)
-        sent, got = "z", ("z", part, k)
-        if k < 3:
-            remote(xs.at[part, ahead, 0], xs.at[part, 2 * k + 2, 0], device(dz=1), sent, got)
-            remote(xs.at[part, behind, 0], xs.at[part, 2 * k + 1, 0], device(dz=-1), sent, got)
-        else:
-            for s, h, d in ((ahead, HALVES[0], 1), (behind, HALVES[1], -1)):
-                remote(xs.at[part, s, 0, :, h], xs.at[part, 7, 0, :, h], device(dz=d), sent, got)
-
-    def z_wait(part, k):
-        wait_got(("z", part, k), xs.at[part, 2 * k + 1:2 * k + 3, 0] if k < 3 else xs.at[part, 7, 0])
+    def z_send(part, k, h):
+        ahead, behind, hh = 2 * k, max(2 * k - 1, 0), HALVES[h]
+        got = ("z", part, k, h)
+        if k < 3 or h == 0:
+            to = 2 * k + 2 if k < 3 else 7
+            remote(xs.at[part, ahead, 0, :, hh], xs.at[part, to, 0, :, hh], device(dz=1), "z", got)
+        if k < 3 or h == 1:
+            remote(xs.at[part, behind, 0, :, hh], xs.at[part, 2 * k + 1, 0, :, hh], device(dz=-1), "z", got)
+
+    def z_wait(part, k, h):
+        hh = HALVES[h]
+        wait_got(("z", part, k, h), xs.at[part, 2 * k + 1:2 * k + 3, 0, :, hh] if k < 3 else xs.at[part, 7, 0, :, hh])
 
     def x_send(part, g):
         zz = pl.ds(GROUPS[g][0], GROUPS[g][1] - GROUPS[g][0])
@@ -200,8 +205,10 @@
         ex[...] = r1[part].astype(F32)
         for j in range(16):
             xs[part, 0, 0, :, j * HD:(j + 1) * HD] = ex[pl.ds(j, 16, stride=16), :].astype(BF16)
-        z_send(part, 0)
+        z_send(part, 0, 0)
         x_send(part, 0)
+    for part in range(2):
+        z_send(part, 0, 1)
 
     def gates(g, i):
         a, b = RUNS[g]
@@ -251,16 +258,29 @@
                 ).reshape(n, 4, 16, 512)
                 un[part, zz, :, cols] = term[:, 0]
                 tb[part, zz, :, :, cols] = term[:, 1:].astype(BF16)
-
-    def depart(g):
+            if g == 2:
+                for one in (2, 3):
+                    depart(part, one)
+                for one in (2, 3):
+                    depart_near(part, one)
+
+    def depart(part, g):
         zz = pl.ds(BACKS[g][0], BACKS[g][1] - BACKS[g][0])
+        for i, d in enumerate((1, -1)):
+            remote(tb.at[part, zz, 2, :, HALVES[i]], fr.at[part, i, zz], along(part, d), "sum", ("relay", part, g))
+
+    def depart_near(part, g):
+        zz = pl.ds(BACKS[g][0], BACKS[g][1] - BACKS[g][0])
+        for i, d in enumerate((1, -1)):
+            h = HALVES[1 - i]
+            remote(tb.at[part, zz, i, :, h], cr.at[part, i, zz, :, h], along(part, d), "sum", ("near", part, g))
+
+    def depart_all(groups):
         for part in range(2):
-            for i, d in enumerate((1, -1)):
-                remote(tb.at[part, zz, 2, :, HALVES[i]], fr.at[part, i, zz], along(part, d), "sum", ("relay", part, g))
-        for part in range(2):
-            for i, d in enumerate((1, -1)):
-                h = HALVES[1 - i]
-                remote(tb.at[part, zz, i, :, h], cr.at[part, i, zz, :, h], along(part, d), "sum", ("near", part, g))
+            for g in groups:
+                depart(part, g)
+            for g in groups:
+                depart_near(part, g)
 
     def relay(g):
         zz = pl.ds(BACKS[g][0], BACKS[g][1] - BACKS[g][0])
@@ -279,11 +299,13 @@
             un[part, zz] = un[part, zz] + (cr[part, 0, zz].astype(F32) + cr[part, 1, zz].astype(F32))
 
     def z_step(k):
-        for part in range(2):
-            z_wait(part, k - 1)
-            if k < 4:
-                z_send(part, k)
-            x_send(part, k)
+        for h in range(2):
+            for part in range(2):
+                z_wait(part, k - 1, h)
+                if k < 4:
+                    z_send(part, k, h)
+                if h == 1:
+                    x_send(part, k)
 
     def forward(g):
         for part in range(2):
@@ -324,27 +346,25 @@
     z_step(4)
     gates(0, 1)
     forward(3)
+    hidden_down(0)
+    forward(4)
+    depart_all((0,))
     gates(1, 0)
-    forward(4)
     gates(1, 1)
-    hidden_down(0)
-    depart(0)
     gates(2, 0)
     gates(2, 1)
     hidden_down(1)
     relay(0)
     hidden_down(2)
-    depart(2)
-    depart(3)
-    collect(0)
     relay(2)
     relay(3)
-    depart(1)
+    depart_all((1,))
+    collect(0)
     collect(2)
     z_sum(0)
+    relay(1)
     collect(3)
     z_sum(1)
-    relay(1)
     collect(1)
     z_sum(2)
     z_sum(3)
@@ -380,7 +400,7 @@
 
 
 N_SEND = 10
-N_RECV = 72
+N_RECV = 80
 
 
 def local(
@@ -393,9 +413,14 @@
     both = pl.pallas_call(
         kernel,
         out_shape=jax.ShapeDtypeStruct((4, 8192), BF16),
-        in_specs=[vmem, vmem, vmem, vmem, smem, vmem] + [hbm] * 5,
+        in_specs=[hbm, hbm, hbm, hbm, smem, hbm] + [hbm] * 5,
         out_specs=vmem,
         scratch_shapes=[
+            pltpu.VMEM((2, 8192), BF16),
+            pltpu.VMEM((2, 8192), BF16),
+            pltpu.VMEM((2, 1024), BF16),
+            pltpu.VMEM((2, 1024), BF16),
+            pltpu.VMEM((64, 128), BF16),
             pltpu.VMEM((2, CACHE, 1024), BF16),
             pltpu.VMEM((2, CACHE, 1024), BF16),
             pltpu.VMEM((2 * UNITS, PLANE), BF16),
@@ -424,7 +449,7 @@
             pltpu.VMEM((2, 2, 4, 32, 128), BF16),
             pltpu.SemaphoreType.DMA((N_SEND,)),
             pltpu.SemaphoreType.DMA((N_RECV,)),
-            pltpu.SemaphoreType.DMA((5,)),
+            pltpu.SemaphoreType.DMA((10,)),
         ],
         compiler_params=pltpu.CompilerParams(
             collective_id=0, has_side_effects=True, vmem_limit_bytes=56 * 2**20

time: 78.4 us -> 76.3 us (0.973)
  Pallas kernels: 76 us -> 73.9 us
    pallas_call x1, Pallas kernels: 76 us -> 73.9 us  [local(): pl.pallas_call(kernel, out_shape=jax.ShapeDtypeStruct((4, 8192), BF16), i...]
where the time goes in v3:
time: 76.3 us; the launch traced here: 76.2 us
  Pallas kernels  73.9 us (97%)
  local copies, waits for them, and re-layouts  1.6 us (2%)
    pallas_call x1, Pallas kernels, local(): pl.pallas_call(kernel, out_shape=jax.ShapeDtypeStruct((4, 8192), BF16), i...  73.9 us
    slice x1, local copies, waits for them, and re-layouts, local(): return (both[:2], both[2:])  1.6 us

profile of v3, /device:TPU:1, one launch (start us, length us, event | category | flops | bytes accessed | tf_op | source)
XLA Modules:
  0.0 76.2 jit_solution(9280866669164938918)
XLA Ops:
  0.6 73.9 %decode_layer.1 = bf16[4,8192]{1,0:T(4,128)(2,1)} custom-call(bf16[2,8192]{1,0:T(2,128)(2,1)} %q_hbm.1, bf16[2,8192]{1,0:T(2,128)(2,1)} %resid_hbm.1, bf16[2,1024]{1,0:T(2,128)(2,1)} %newk_hbm.1, bf16[2,1024]{1,0:T(2,128)(2,1)} %newv_hbm.1, s32[2]{0:T(128)} %len_ref.1, bf16[64,128]{1,0:T(8,128)(2,1)} %bitcast.1, bf16[2,192,1024]{2,1,0:T(8,128)(2,1)} %k_hbm.1, ...), custom_call_target="tpu_custom_call" | custom-call | tf_op jit(solution)/shard_map/decode_layer/pallas_call | solution.py:413
  74.6 1.6 %fusion = (bf16[2,8192]{1,0:T(2,128)(2,1)}, bf16[2,8192]{1,0:T(2,128)(2,1)}) fusion(bf16[4,8192]{1,0:T(4,128)(2,1)} %decode_layer.1), kind=kLoop, calls=%fused_computation | loop fusion | bytes 131072 | tf_op jit(solution)/shard_map/slice | solution.py:462
